TPU v7x, 32 devices: a whole 2x2x4 slice. The times are simulated.
32 devices in a mesh: rep: 4 (over y, x), shard: 8 (over z, core).
Axes of the slice: x: 2, y: 2, z: 4, core: 2. Of those that a mesh axis runs over, the one named last changes fastest.
Arguments:
- tokens: bfloat16 [32768, 768], P(('rep', 'shard')), may hold values from -6 to 6
- cotangent: bfloat16 [32768, 768], P(('rep', 'shard')), may hold values from -6 to 6
- seq_lengths: int32 [128], P(('rep', 'shard')), may hold values from 0 to 1024, as said below
- seq_blocks: int32 [128], P(('rep', 'shard')), may hold values from 0 to 8, as said below
- ln1_gain: bfloat16 [768], P('shard'), may hold values from 0.25 to 1.75
- ln1_bias: bfloat16 [768], P('shard'), may hold values from -3 to 3
- w_qkv: bfloat16 [768, 2304], P('shard'), may hold values from -0.21875 to 0.21875
- q_bias: bfloat16 [768], P('shard'), may hold values from -3 to 3
- v_bias: bfloat16 [768], P('shard'), may hold values from -3 to 3
- w_out: bfloat16 [768, 768], P('shard'), may hold values from -0.875 to 0.875
- out_bias: bfloat16 [768], P('shard'), may hold values from -3 to 3
- ln2_gain: bfloat16 [768], P('shard'), may hold values from 0.25 to 1.75
- ln2_bias: bfloat16 [768], P('shard'), may hold values from -3 to 3
- w_fc: bfloat16 [768, 3072], P('shard'), may hold values from -0.21875 to 0.21875
- fc_bias: bfloat16 [3072], P('shard'), may hold values from -3 to 3
- w_proj: bfloat16 [3072, 768], P('shard'), may hold values from -0.15625 to 0.15625
- proj_bias: bfloat16 [768], P('shard'), may hold values from -3 to 3
Outputs:
- output: bfloat16 [32768, 768], P(('rep', 'shard'))
- token_grad: bfloat16 [32768, 768], P(('rep', 'shard'))
- ln1_gain_grad: float32 [768], P('shard')
- ln1_bias_grad: float32 [768], P('shard')
- w_qkv_grad: float32 [768, 2304], P('shard')
- q_bias_grad: float32 [768], P('shard')
- v_bias_grad: float32 [768], P('shard')
- w_out_grad: float32 [768, 768], P('shard')
- out_bias_grad: float32 [768], P('shard')
- ln2_gain_grad: float32 [768], P('shard')
- ln2_bias_grad: float32 [768], P('shard')
- w_fc_grad: float32 [768, 3072], P('shard')
- fc_bias_grad: float32 [3072], P('shard')
- w_proj_grad: float32 [3072, 768], P('shard')
- proj_bias_grad: float32 [768], P('shard')
Inputs may be any that keep to these rules, and one draw needn't show every extreme that they name: `seq_lengths`: entries come in groups of 4, one group a device in the order of its index along rep+shard. Slot lengths are 0 for empty slots; a slot's tokens start at 128 times its entry of seq_blocks, the slots of a device follow each other without intersection and stay within its 1024 tokens. In every draw some device holds one sequence of 1024 tokens. `seq_blocks`: block offsets of a device's slots never fall; an empty slot's offset equals the end of the slots before it.
All inputs are finite; a program needn't handle non-finite values.
Results may differ from a plain program's by a relative error of at most 0.015.
Values may be sent and summed in bfloat16 or wider, within the bound.
No kernel may reach another device: no remote copies, remote signals or barrier semaphores. Data moves between devices by JAX's collectives and lax.ppermute only.
A program may use at most 256 MiB of HBM per device.

v0:
```python
import jax
import jax.numpy as jnp
from jax import lax
from jax.sharding import PartitionSpec as P

HEADS = 12
HEAD_DIM = 64
BLOCK = 128


def layer_norm(values, gain_vec, bias_vec):
    average = jnp.mean(values, axis=-1, keepdims=True)
    centred = values - average
    variance = jnp.mean(centred * centred, axis=-1, keepdims=True)
    return centred * lax.rsqrt(variance + 1e-05) * gain_vec + bias_vec


def gelu_tanh(values):
    return jax.nn.gelu(values, approximate=True)


def segments(lengths, offsets, rows_here, block_size):
    positions = jnp.arange(rows_here, dtype=jnp.int32)
    starts_at = offsets * block_size
    ends_at = starts_at + lengths
    inside = (positions[None, :] >= starts_at[:, None]) & (positions[None, :] < ends_at[:, None])
    slot_ids = jnp.arange(lengths.shape[0], dtype=jnp.int32)
    seg_ids = jnp.sum(jnp.where(inside, slot_ids[:, None], 0), axis=0)
    live_mask = jnp.any(inside, axis=0)
    seg_ids = jnp.where(live_mask, seg_ids, -1 - positions)
    return (seg_ids, live_mask)


def contract_rows(left, right):
    return lax.dot_general(
        left, right, (((0,), (0,)), ((), ())), preferred_element_type=jnp.float32
    )


def times_transposed(left, right):
    return lax.dot_general(
        left, right, (((1,), (1,)), ((), ())), preferred_element_type=jnp.float32
    )


def local(
    tokens,
    cotangent,
    seq_lengths,
    seq_blocks,
    ln1_gain,
    ln1_bias,
    w_qkv,
    q_bias,
    v_bias,
    w_out,
    out_bias,
    ln2_gain,
    ln2_bias,
    w_fc,
    fc_bias,
    w_proj,
    proj_bias,
):
    rows_here = tokens.shape[0]
    model_width = tokens.shape[1]
    head_count = HEADS
    head_size = HEAD_DIM
    factor = float(HEAD_DIM) ** (-0.5)
    seg_ids, live_mask = segments(seq_lengths, seq_blocks, rows_here, BLOCK)
    positions = jnp.arange(rows_here, dtype=jnp.int32)
    row_block = min(512, rows_here)
    block_count = rows_here // row_block
    block_starts = jnp.arange(block_count, dtype=jnp.int32) * row_block
    gain_one, bias_one, qkv_weight, query_shift, value_shift, out_weight, out_shift = (
        lax.all_gather(ln1_gain, "shard", axis=0, tiled=True),
        lax.all_gather(ln1_bias, "shard", axis=0, tiled=True),
        lax.all_gather(w_qkv, "shard", axis=0, tiled=True),
        lax.all_gather(q_bias, "shard", axis=0, tiled=True),
        lax.all_gather(v_bias, "shard", axis=0, tiled=True),
        lax.all_gather(w_out, "shard", axis=0, tiled=True),
        lax.all_gather(out_bias, "shard", axis=0, tiled=True),
    )
    inputs_f = tokens.astype(jnp.float32)
    h_one = layer_norm(inputs_f, gain_one.astype(jnp.float32), bias_one.astype(jnp.float32)).astype(
        jnp.bfloat16
    )
    qkv_shift = jnp.concatenate(
        [
            query_shift.astype(jnp.float32),
            jnp.zeros((model_width,), jnp.float32),
            value_shift.astype(jnp.float32),
        ]
    )
    qkv_low = (jnp.dot(h_one, qkv_weight, preferred_element_type=jnp.float32) + qkv_shift).astype(
        jnp.bfloat16
    )
    queries = qkv_low[:, :model_width].reshape(rows_here, head_count, head_size)
    keys_all = qkv_low[:, model_width : 2 * model_width].reshape(rows_here, head_count, head_size)
    values_all = qkv_low[:, 2 * model_width :].reshape(rows_here, head_count, head_size)
    query_blocks = queries.reshape(block_count, row_block, head_count, head_size)

    def block_scores(query_rows, row_start):
        scores = (
            jnp.einsum("qhd,khd->hqk", query_rows, keys_all, preferred_element_type=jnp.float32)
            * factor
        )
        row_seg = lax.dynamic_slice_in_dim(seg_ids, row_start, row_block)
        row_pos = row_start + jnp.arange(row_block, dtype=jnp.int32)
        allowed = (row_seg[:, None] == seg_ids[None, :]) & (positions[None, :] <= row_pos[:, None])
        return (scores, allowed)

    def forward_block(block_item):
        query_rows, row_start = block_item
        scores, allowed = block_scores(query_rows, row_start)
        scores = jnp.where(allowed[None], scores, -1e30)
        largest = jnp.max(scores, axis=-1, keepdims=True)
        totals = jnp.sum(jnp.exp(scores - largest), axis=-1, keepdims=True)
        log_total = largest + jnp.log(totals)
        weights_low = jnp.exp(scores - log_total).astype(jnp.bfloat16)
        mixed_rows = jnp.einsum(
            "hqk,khd->qhd", weights_low, values_all, preferred_element_type=jnp.float32
        )
        return (mixed_rows, log_total[..., 0])

    mixed_blocks, log_totals = lax.map(forward_block, (query_blocks, block_starts))
    attn_low = mixed_blocks.reshape(rows_here, model_width).astype(jnp.bfloat16)
    residual = (
        inputs_f
        + jnp.dot(attn_low, out_weight, preferred_element_type=jnp.float32)
        + out_shift.astype(jnp.float32)
    )
    gain_two, bias_two, fc_weight, fc_shift, proj_weight, proj_shift = (
        lax.all_gather(ln2_gain, "shard", axis=0, tiled=True),
        lax.all_gather(ln2_bias, "shard", axis=0, tiled=True),
        lax.all_gather(w_fc, "shard", axis=0, tiled=True),
        lax.all_gather(fc_bias, "shard", axis=0, tiled=True),
        lax.all_gather(w_proj, "shard", axis=0, tiled=True),
        lax.all_gather(proj_bias, "shard", axis=0, tiled=True),
    )
    h_two = layer_norm(residual, gain_two.astype(jnp.float32), bias_two.astype(jnp.float32)).astype(
        jnp.bfloat16
    )
    pre_act = jnp.dot(h_two, fc_weight, preferred_element_type=jnp.float32) + fc_shift.astype(
        jnp.float32
    )
    act_low = gelu_tanh(pre_act).astype(jnp.bfloat16)
    output = (
        residual
        + jnp.dot(act_low, proj_weight, preferred_element_type=jnp.float32)
        + proj_shift.astype(jnp.float32)
    ).astype(jnp.bfloat16)
    gain_back, fc_back, proj_back = (
        lax.all_gather(ln2_gain, "shard", axis=0, tiled=True),
        lax.all_gather(w_fc, "shard", axis=0, tiled=True),
        lax.all_gather(w_proj, "shard", axis=0, tiled=True),
    )
    upstream = cotangent.astype(jnp.float32) * live_mask[:, None].astype(jnp.float32)
    back_mlp = upstream.astype(jnp.bfloat16)
    grad_proj = contract_rows(act_low, back_mlp)
    grad_proj_shift = jnp.sum(back_mlp.astype(jnp.float32), axis=0)
    back_act = times_transposed(back_mlp, proj_back)
    gelu_pull = jax.vjp(gelu_tanh, pre_act)[1]
    back_pre = gelu_pull(back_act)[0].astype(jnp.bfloat16)
    grad_fc = contract_rows(h_two, back_pre)
    grad_fc_shift = jnp.sum(back_pre.astype(jnp.float32), axis=0)
    back_htwo = times_transposed(back_pre, fc_back)
    zero_bias = jnp.zeros((model_width,), jnp.float32)
    norm_two_pull = jax.vjp(layer_norm, residual, gain_back.astype(jnp.float32), zero_bias)[1]
    back_resid_norm, grad_gain_two, grad_bias_two = norm_two_pull(back_htwo)
    back_resid = upstream + back_resid_norm
    mlp_sums = (
        lax.psum_scatter(grad_gain_two, "shard", scatter_dimension=0, tiled=True),
        lax.psum_scatter(grad_bias_two, "shard", scatter_dimension=0, tiled=True),
        lax.psum_scatter(grad_fc, "shard", scatter_dimension=0, tiled=True),
        lax.psum_scatter(grad_fc_shift, "shard", scatter_dimension=0, tiled=True),
        lax.psum_scatter(grad_proj, "shard", scatter_dimension=0, tiled=True),
        lax.psum_scatter(grad_proj_shift, "shard", scatter_dimension=0, tiled=True),
    )
    gain_first, qkv_back, out_back = (
        lax.all_gather(ln1_gain, "shard", axis=0, tiled=True),
        lax.all_gather(w_qkv, "shard", axis=0, tiled=True),
        lax.all_gather(w_out, "shard", axis=0, tiled=True),
    )
    back_branch = back_resid.astype(jnp.bfloat16)
    grad_out = contract_rows(attn_low, back_branch)
    grad_out_shift = jnp.sum(back_branch.astype(jnp.float32), axis=0)
    back_attn = times_transposed(back_branch, out_back).astype(jnp.bfloat16)
    back_attn = back_attn.reshape(block_count, row_block, head_count, head_size)

    def backward_block(carried, block_item):
        key_grad, value_grad = carried
        query_rows, upstream_rows, log_rows, row_start = block_item
        scores, allowed = block_scores(query_rows, row_start)
        weights_f = jnp.where(allowed[None], jnp.exp(scores - log_rows[..., None]), 0.0)
        weights_low = weights_f.astype(jnp.bfloat16)
        value_grad = value_grad + jnp.einsum(
            "hqk,qhd->khd", weights_low, upstream_rows, preferred_element_type=jnp.float32
        )
        back_weights = jnp.einsum(
            "qhd,khd->hqk", upstream_rows, values_all, preferred_element_type=jnp.float32
        )
        inner_sum = jnp.sum(weights_f * back_weights, axis=-1, keepdims=True)
        back_scores = (weights_f * (back_weights - inner_sum)).astype(jnp.bfloat16)
        query_grad = (
            jnp.einsum("hqk,khd->qhd", back_scores, keys_all, preferred_element_type=jnp.float32)
            * factor
        )
        key_grad = (
            key_grad
            + jnp.einsum(
                "hqk,qhd->khd", back_scores, query_rows, preferred_element_type=jnp.float32
            )
            * factor
        )
        return ((key_grad, value_grad), query_grad)

    zero_heads = jnp.zeros((rows_here, head_count, head_size), jnp.float32)
    (key_grad, value_grad), query_grads = lax.scan(
        backward_block,
        (zero_heads, zero_heads),
        (query_blocks, back_attn, log_totals, block_starts),
    )
    back_qkv = jnp.concatenate(
        [
            query_grads.reshape(rows_here, model_width),
            key_grad.reshape(rows_here, model_width),
            value_grad.reshape(rows_here, model_width),
        ],
        axis=1,
    ).astype(jnp.bfloat16)
    grad_qkv = contract_rows(h_one, back_qkv)
    qkv_column_sums = jnp.sum(back_qkv.astype(jnp.float32), axis=0)
    grad_query_shift = qkv_column_sums[:model_width]
    grad_value_shift = qkv_column_sums[2 * model_width :]
    back_hone = times_transposed(back_qkv, qkv_back)
    norm_one_pull = jax.vjp(layer_norm, inputs_f, gain_first.astype(jnp.float32), zero_bias)[1]
    back_input_norm, grad_gain_one, grad_bias_one = norm_one_pull(back_hone)
    token_grad = (back_resid + back_input_norm).astype(jnp.bfloat16)
    attn_sums = (
        lax.psum_scatter(grad_gain_one, "shard", scatter_dimension=0, tiled=True),
        lax.psum_scatter(grad_bias_one, "shard", scatter_dimension=0, tiled=True),
        lax.psum_scatter(grad_qkv, "shard", scatter_dimension=0, tiled=True),
        lax.psum_scatter(grad_query_shift, "shard", scatter_dimension=0, tiled=True),
        lax.psum_scatter(grad_value_shift, "shard", scatter_dimension=0, tiled=True),
        lax.psum_scatter(grad_out, "shard", scatter_dimension=0, tiled=True),
        lax.psum_scatter(grad_out_shift, "shard", scatter_dimension=0, tiled=True),
    )
    summed = (
        lax.psum(attn_sums[0].astype(jnp.bfloat16), "rep").astype(jnp.float32),
        lax.psum(attn_sums[1].astype(jnp.bfloat16), "rep").astype(jnp.float32),
        lax.psum(attn_sums[2].astype(jnp.bfloat16), "rep").astype(jnp.float32),
        lax.psum(attn_sums[3].astype(jnp.bfloat16), "rep").astype(jnp.float32),
        lax.psum(attn_sums[4].astype(jnp.bfloat16), "rep").astype(jnp.float32),
        lax.psum(attn_sums[5].astype(jnp.bfloat16), "rep").astype(jnp.float32),
        lax.psum(attn_sums[6].astype(jnp.bfloat16), "rep").astype(jnp.float32),
        lax.psum(mlp_sums[0].astype(jnp.bfloat16), "rep").astype(jnp.float32),
        lax.psum(mlp_sums[1].astype(jnp.bfloat16), "rep").astype(jnp.float32),
        lax.psum(mlp_sums[2].astype(jnp.bfloat16), "rep").astype(jnp.float32),
        lax.psum(mlp_sums[3].astype(jnp.bfloat16), "rep").astype(jnp.float32),
        lax.psum(mlp_sums[4].astype(jnp.bfloat16), "rep").astype(jnp.float32),
        lax.psum(mlp_sums[5].astype(jnp.bfloat16), "rep").astype(jnp.float32),
    )
    return (
        output,
        token_grad,
        summed[0],
        summed[1],
        summed[2],
        summed[3],
        summed[4],
        summed[5],
        summed[6],
        summed[7],
        summed[8],
        summed[9],
        summed[10],
        summed[11],
        summed[12],
    )


def solution(mesh):
    placed = (
        P(("rep", "shard"), None),
        P(("rep", "shard"), None),
        P(("rep", "shard")),
        P(("rep", "shard")),
        P("shard"),
        P("shard"),
        P("shard", None),
        P("shard"),
        P("shard"),
        P("shard", None),
        P("shard"),
        P("shard"),
        P("shard"),
        P("shard", None),
        P("shard"),
        P("shard", None),
        P("shard"),
    )
    return jax.shard_map(
        local,
        mesh=mesh,
        in_specs=placed,
        out_specs=(
            P(("rep", "shard"), None),
            P(("rep", "shard"), None),
            P("shard"),
            P("shard"),
            P("shard", None),
            P("shard"),
            P("shard"),
            P("shard", None),
            P("shard"),
            P("shard"),
            P("shard"),
            P("shard", None),
            P("shard"),
            P("shard", None),
            P("shard"),
        ),
        check_vma=False,
    )
```

profile of v0, /device:TPU:0, one launch (start us, length us, event | category | flops | bytes accessed | tf_op | source)
XLA Modules:
  0.0 795.5 jit_solution(3468339074451375724)
XLA Ops:
  20.3 31.6 %all-reduce.18 = (bf16[768]{0:T(1024)(128)(2,1)S(1)}, bf16[768]{0:T(1024)(128)(2,1)S(1)}, bf16[768]{0:T(1024)(128)(2,1)S(1)}, bf16[768]{0:T(1024)(128)(2,1)S(1)}...) all-reduce(bf16[768]{0:T(1024)(128)(2,1)S(1)} %dynamic-update-slice, ...), channel_id=1, replica_groups=mesh['rep'=4,'shard'=8] {'shard'}, use_global_device_ids=true, to_apply=%add.3 | all-reduce | flops 6144 | bytes 24576
  54.3 12.7 %all-gather = bf16[8,1,384]{2,1,0:T(2,128)(2,1)S(1)} all-gather(bf16[1,1,384]{2,1,0:T(2,128)(2,1)S(1)} %reshape.306), channel_id=1, replica_groups=mesh['rep'=4,'shard'=8] {'shard'}, dimensions={0}, use_global_device_ids=true | all-gather | bytes 6912 | tf_op jit(solution)/shard_map/all_gather | solution.py:137
  91.8 79.0 %while.28 = (s32[]{:T(128)}, bf16[2,512,12,64]{1,3,2,0:T(8,128)(2,1)}, f32[2,12,512]{2,1,0:T(8,128)S(1)}, s32[2]{0:T(128)S(1)}, s32[1024]{0:T(1024)S(1)}, /*inde...) while((s32[]{:T(128)}, ...), condition=%wide.region_7.8_spmd.clone, body=%wide.region_4.7_spmd.clone.sunk | while | flops 1681385984 | bytes 102226184 | solution.py:126
  95.8 10.9 %fusion.121 = (f32[12,512]{1,0:T(8,128)S(1)}, f32[12,512,1024]{2,1,0:T(8,128)}) fusion(pred[512,1024]{1,0:T(8,128)(4,1)S(1)} %fusion.120, bf16[1024,12,64]{0,2,1:T(8,128)(2,1)S(1)} %get-tuple-element.580, bf16[2,512,12,64]{1,3,2,0:T(8,128)(2,1)S(1)} %get-tuple-element.579, s32[]{:T(128)S(6)} %copy.119), kind=kOutput, calls=%fused_computation.5.clone.1 | convolution fusion | flops 824174592 | bytes 28073988 | tf_op jit(solution)/shard_map/while/body/eval_jaxpr/qhd,khd->hqk/dot_general | solution.py:105
  106.7 12.1 %exponential_reduce_fusion.2 = f32[12,512]{1,0:T(8,128)S(1)} fusion(f32[12,512,1024]{2,1,0:T(8,128)} %get-tuple-element.535, f32[12,512]{1,0:T(8,128)S(1)} %get-tuple-element.536, pred[512,1024]{1,0:T(8,128)(4,1)S(1)} %fusion.120), kind=kLoop, calls=%fused_computation.3.clone.1 | loop fusion | flops 25159680 | bytes 25739264 | tf_op jit(solution)/shard_map/while/body/eval_jaxpr/reduce_sum | solution.py:118
  118.9 11.3 %bitcast_dynamic-update-slice_fusion.7 = bf16[2,512,12,64]{1,3,2,0:T(8,128)(2,1)S(1)} fusion(bf16[2,512,12,64]{1,3,2,0:T(8,128)(2,1)S(1)} %copy-done.14, s32[]{:T(128)S(6)} %copy.119, bf16[1024,12,64]{0,2,1:T(8,128)(2,1)S(1)} %copy-done.3, f32[12,512,1024]{2,1,0:T(8,128)} %get-tuple-element.535, f32[12,512]{1,0:T(8,128)S(1)} %get-tuple-element.537, ...), kind=kOutput, calls=%fused_computation.10.clone.1 | convolution fusion | flops 830472192 | bytes 28868612 | tf_op jit(solution)/shard_map/while/body/eval_jaxpr/hqk,khd->qhd/dot_general | solution.py:121
  135.2 11.0 %fusion.121 = (f32[12,512]{1,0:T(8,128)S(1)}, f32[12,512,1024]{2,1,0:T(8,128)}) fusion(pred[512,1024]{1,0:T(8,128)(4,1)S(1)} %fusion.120, bf16[1024,12,64]{0,2,1:T(8,128)(2,1)S(1)} %get-tuple-element.580, bf16[2,512,12,64]{1,3,2,0:T(8,128)(2,1)S(1)} %get-tuple-element.579, s32[]{:T(128)S(6)} %copy.119), kind=kOutput, calls=%fused_computation.5.clone.1 | convolution fusion | flops 824174592 | bytes 28073988 | tf_op jit(solution)/shard_map/while/body/eval_jaxpr/qhd,khd->hqk/dot_general | solution.py:105
  146.2 12.1 %exponential_reduce_fusion.2 = f32[12,512]{1,0:T(8,128)S(1)} fusion(f32[12,512,1024]{2,1,0:T(8,128)} %get-tuple-element.535, f32[12,512]{1,0:T(8,128)S(1)} %get-tuple-element.536, pred[512,1024]{1,0:T(8,128)(4,1)S(1)} %fusion.120), kind=kLoop, calls=%fused_computation.3.clone.1 | loop fusion | flops 25159680 | bytes 25739264 | tf_op jit(solution)/shard_map/while/body/eval_jaxpr/reduce_sum | solution.py:118
  158.3 11.4 %bitcast_dynamic-update-slice_fusion.7 = bf16[2,512,12,64]{1,3,2,0:T(8,128)(2,1)S(1)} fusion(bf16[2,512,12,64]{1,3,2,0:T(8,128)(2,1)S(1)} %copy-done.14, s32[]{:T(128)S(6)} %copy.119, bf16[1024,12,64]{0,2,1:T(8,128)(2,1)S(1)} %copy-done.3, f32[12,512,1024]{2,1,0:T(8,128)} %get-tuple-element.535, f32[12,512]{1,0:T(8,128)S(1)} %get-tuple-element.537, ...), kind=kOutput, calls=%fused_computation.10.clone.1 | convolution fusion | flops 830472192 | bytes 28868612 | tf_op jit(solution)/shard_map/while/body/eval_jaxpr/hqk,khd->qhd/dot_general | solution.py:121
  181.6 11.2 %fusion.72 = f32[1024,3072]{1,0:T(8,128)} fusion(bf16[768,3072]{1,0:T(8,128)(2,1)} %all-gather.10.cloned.1.call-done, f32[1024,768]{0,1:T(8,128)} %copy-done.6, f32[768]{0:T(1024)S(1)} %copy-done.30, f32[768]{0:T(1024)S(1)} %copy-done.26, f32[1024]{0:T(1024)S(1)} %fusion.64, f32[1024]{0:T(1024)S(1)} %broadcast_multiply_fusion), kind=kOutput, calls=%fused_computation.127 | convolution fusion | flops 4835770368 | bytes 20461568 | tf_op jit(solution)/shard_map/dot_general | solution.py:144
  192.9 17.7 %convert_reduce_fusion = (f32[3072]{0:T(1024)}, bf16[1024,3072]{1,0:T(8,128)(2,1)S(1)}) fusion(f32[1024,3072]{1,0:T(8,128)} %fusion.72, f32[3072]{0:T(1024)S(1)} %bitcast.132, bf16[3072,768]{1,0:T(8,128)(2,1)} %all-gather.12.cloned.1.call-done, bf16[1024,768]{0,1:T(8,128)(2,1)} %copy.91, f32[1024]{0:T(1024)S(1)} %copy-done.36), kind=kOutput, calls=%fused_computation.58 | convolution fusion | flops 4906546176 | bytes 25194496 | tf_op jit(solution)/shard_map/dot_general | solution.py:41
  248.0 174.2 %while.29 = (s32[]{:T(128)}, f32[1024,12,64]{0,2,1:T(8,128)}, f32[1024,12,64]{0,2,1:T(8,128)}, bf16[2,512,12,64]{1,3,2,0:T(8,128)(2,1)}, bf16[2,512,12,64]{1,3,2...) while((s32[]{:T(128)}, f32[1024,12,64]{0,2,1:T(8,128)}, ...), condition=%wide.region_14.15_spmd.clone, body=%wide.region_12.14_spmd.clone.sunk | while | flops 4126796288 | bytes 231930176 | solution.py:219
  252.1 11.6 %fusion.131 = f32[12,512,1024]{2,1,0:T(8,128)} fusion(bf16[1024,12,64]{0,2,1:T(8,128)(2,1)S(1)} %get-tuple-element.620, bf16[2,512,12,64]{1,3,2,0:T(8,128)(2,1)} %copy-done.1, s32[]{:T(128)S(6)} %copy.129), kind=kOutput, calls=%fused_computation.35.clone.1 | convolution fusion | flops 805306368 | bytes 27525124 | tf_op jit(solution)/shard_map/while/body/eval_jaxpr/qhd,khd->hqk/dot_general | solution.py:105
  263.7 13.0 %bitcast_add_fusion.5 = f32[1024,12,64]{0,2,1:T(8,128)} fusion(f32[1024,12,64]{0,2,1:T(8,128)} %get-tuple-element.601, f32[12,512,1024]{2,1,0:T(8,128)} %fusion.131, f32[12,512]{1,0:T(8,128)S(1)} %dynamic-slice_bitcast_fusion.2, pred[512,1024]{1,0:T(8,128)(4,1)S(1)} %fusion.132, pred[]{:T(512)S(6)} %compare.3, ...), kind=kOutput, calls=%fused_computation.26.clone.1 | convolution fusion | flops 832045056 | bytes 32800772 | tf_op jit(solution)/shard_map/while/body/eval_jaxpr/hqk,qhd->khd/dot_general | solution.py:197
  276.8 18.3 %multiply_reduce_fusion.5 = (f32[12,512]{1,0:T(8,128)S(1)}, f32[12,512,1024]{2,1,0:T(8,128)}) fusion(f32[12,512,1024]{2,1,0:T(8,128)} %fusion.131, f32[12,512]{1,0:T(8,128)S(1)} %dynamic-slice_bitcast_fusion.2, pred[512,1024]{1,0:T(8,128)(4,1)S(1)} %fusion.132, bf16[1024,12,64]{0,2,1:T(8,128)(2,1)} %get-tuple-element.623, ...), kind=kOutput, calls=%fused_computation.21.clone.1 | convolution fusion | flops 836757504 | bytes 53264388 | tf_op jit(solution)/shard_map/while/body/eval_jaxpr/qhd,khd->hqk/dot_general | solution.py:200
  295.1 21.2 %multiply_convert_fusion.5 = bf16[12,512,1024]{2,1,0:T(8,128)(2,1)} fusion(f32[12,512,1024]{2,1,0:T(8,128)} %get-tuple-element.550, f32[12,512,1024]{2,1,0:T(8,128)} %fusion.131, f32[12,512]{1,0:T(8,128)S(1)} %get-tuple-element.551, f32[12,512]{1,0:T(8,128)S(1)} %dynamic-slice_bitcast_fusion.2, pred[512,1024]{1,0:T(8,128)(4,1)S(1)} %fusion.132), kind=kLoop, calls=%fused_computation.20.clone.1 | loop fusion | flops 37748736 | bytes 63488000 | tf_op jit(solution)/shard_map/while/body/eval_jaxpr/convert_element_type | solution.py:204
  316.2 9.5 %bitcast_dynamic-update-slice_fusion.8 = bf16[2,512,12,64]{1,3,2,0:T(8,128)(2,1)} fusion(bf16[2,512,12,64]{1,3,2,0:T(8,128)(2,1)} %get-tuple-element.602, s32[]{:T(128)S(6)} %copy.129, bf16[12,512,1024]{2,1,0:T(8,128)(2,1)} %multiply_convert_fusion.5, bf16[1024,12,64]{0,2,1:T(8,128)(2,1)S(1)} %get-tuple-element.620), kind=kOutput, calls=%fused_computation.30.clone.1 | convolution fusion | flops 805699584 | bytes 15728644 | tf_op jit(solution)/shard_map/while/body/eval_jaxpr/hqk,khd->qhd/dot_general | solution.py:206
  338.3 11.4 %fusion.131 = f32[12,512,1024]{2,1,0:T(8,128)} fusion(bf16[1024,12,64]{0,2,1:T(8,128)(2,1)S(1)} %get-tuple-element.620, bf16[2,512,12,64]{1,3,2,0:T(8,128)(2,1)} %copy-done.1, s32[]{:T(128)S(6)} %copy.129), kind=kOutput, calls=%fused_computation.35.clone.1 | convolution fusion | flops 805306368 | bytes 27525124 | tf_op jit(solution)/shard_map/while/body/eval_jaxpr/qhd,khd->hqk/dot_general | solution.py:105
  349.7 13.7 %bitcast_add_fusion.5 = f32[1024,12,64]{0,2,1:T(8,128)} fusion(f32[1024,12,64]{0,2,1:T(8,128)} %get-tuple-element.601, f32[12,512,1024]{2,1,0:T(8,128)} %fusion.131, f32[12,512]{1,0:T(8,128)S(1)} %dynamic-slice_bitcast_fusion.2, pred[512,1024]{1,0:T(8,128)(4,1)S(1)} %fusion.132, pred[]{:T(512)S(6)} %compare.3, ...), kind=kOutput, calls=%fused_computation.26.clone.1 | convolution fusion | flops 832045056 | bytes 32800772 | tf_op jit(solution)/shard_map/while/body/eval_jaxpr/hqk,qhd->khd/dot_general | solution.py:197
  363.4 18.2 %multiply_reduce_fusion.5 = (f32[12,512]{1,0:T(8,128)S(1)}, f32[12,512,1024]{2,1,0:T(8,128)}) fusion(f32[12,512,1024]{2,1,0:T(8,128)} %fusion.131, f32[12,512]{1,0:T(8,128)S(1)} %dynamic-slice_bitcast_fusion.2, pred[512,1024]{1,0:T(8,128)(4,1)S(1)} %fusion.132, bf16[1024,12,64]{0,2,1:T(8,128)(2,1)} %get-tuple-element.623, ...), kind=kOutput, calls=%fused_computation.21.clone.1 | convolution fusion | flops 836757504 | bytes 53264388 | tf_op jit(solution)/shard_map/while/body/eval_jaxpr/qhd,khd->hqk/dot_general | solution.py:200
  381.6 21.2 %multiply_convert_fusion.5 = bf16[12,512,1024]{2,1,0:T(8,128)(2,1)} fusion(f32[12,512,1024]{2,1,0:T(8,128)} %get-tuple-element.550, f32[12,512,1024]{2,1,0:T(8,128)} %fusion.131, f32[12,512]{1,0:T(8,128)S(1)} %get-tuple-element.551, f32[12,512]{1,0:T(8,128)S(1)} %dynamic-slice_bitcast_fusion.2, pred[512,1024]{1,0:T(8,128)(4,1)S(1)} %fusion.132), kind=kLoop, calls=%fused_computation.20.clone.1 | loop fusion | flops 37748736 | bytes 63488000 | tf_op jit(solution)/shard_map/while/body/eval_jaxpr/convert_element_type | solution.py:204
  402.7 9.5 %bitcast_dynamic-update-slice_fusion.8 = bf16[2,512,12,64]{1,3,2,0:T(8,128)(2,1)} fusion(bf16[2,512,12,64]{1,3,2,0:T(8,128)(2,1)} %get-tuple-element.602, s32[]{:T(128)S(6)} %copy.129, bf16[12,512,1024]{2,1,0:T(8,128)(2,1)} %multiply_convert_fusion.5, bf16[1024,12,64]{0,2,1:T(8,128)(2,1)S(1)} %get-tuple-element.620), kind=kOutput, calls=%fused_computation.30.clone.1 | convolution fusion | flops 805699584 | bytes 15728644 | tf_op jit(solution)/shard_map/while/body/eval_jaxpr/hqk,khd->qhd/dot_general | solution.py:206
  412.2 9.5 %bitcast_add_fusion.4 = f32[1024,12,64]{0,2,1:T(8,128)} fusion(f32[1024,12,64]{0,2,1:T(8,128)} %get-tuple-element.600, bf16[12,512,1024]{2,1,0:T(8,128)(2,1)} %multiply_convert_fusion.5, pred[]{:T(512)S(6)} %compare.3, bf16[2,512,12,64]{1,3,2,0:T(8,128)(2,1)S(1)} %copy-done.2, s32[]{:T(128)S(6)} %copy.129), kind=kOutput, calls=%fused_computation.27.clone.1 | convolution fusion | flops 807665664 | bytes 19660804 | tf_op jit(solution)/shard_map/while/body/eval_jaxpr/hqk,qhd->khd/dot_general | solution.py:211
  438.7 13.9 %fusion.58 = f32[3072,768]{1,0:T(8,128)} fusion(bf16[1024,768]{0,1:T(8,128)(2,1)S(1)} %copy-done.13, f32[1024]{0:T(1024)S(1)} %copy-done.37, f32[1024,3072]{1,0:T(8,128)} %fusion.72, f32[3072]{0:T(1024)S(1)} %bitcast.133), kind=kOutput, calls=%fused_computation.93 | convolution fusion | flops 4865654784 | bytes 23609344 | tf_op jit(solution)/shard_map/dot_general | solution.py:35
  453.3 10.9 %fusion.71 = f32[768,3072]{1,0:T(8,128)} fusion(bf16[1024,3072]{1,0:T(8,128)(2,1)} %copy-done.55, f32[1024,768]{0,1:T(8,128)} %copy-done.6, f32[768]{0:T(1024)S(1)} %copy-done.31, f32[768]{0:T(1024)S(1)} %copy-done.27, f32[1024]{0:T(1024)S(1)} %copy-done.29, f32[1024]{0:T(1024)S(1)} %copy-done.25), kind=kOutput, calls=%fused_computation.126 | convolution fusion | flops 4835770368 | bytes 18888704 | tf_op jit(solution)/shard_map/dot_general | solution.py:35
  465.6 9.0 %fusion.79 = (f32[768]{0:T(1024)S(1)}, f32[1024,768]{1,0:T(8,128)}) fusion(bf16[768,2304]{1,0:T(8,128)(2,1)} %all-gather.6.cloned.1.call-done, bf16[1024,768]{0,1:T(8,128)(2,1)} %bitcast.128, bf16[1024,768]{0,1:T(8,128)(2,1)} %bitcast.125, bf16[1024,768]{0,1:T(8,128)(2,1)} %bitcast.122), kind=kOutput, calls=%fused_computation.133 | convolution fusion | flops 3638820096 | bytes 11406336 | tf_op jit(solution)/shard_map/dot_general | solution.py:41
  481.7 11.9 %add_convert_fusion.2 = bf16[1024,768]{0,1:T(8,128)(2,1)} fusion(f32[1024,768]{0,1:T(8,128)S(1)} %copy-done.8, bf16[3072,768]{1,0:T(8,128)(2,1)} %all-gather.12.cloned.1.call-done, f32[768]{0:T(1024)S(1)} %convert_element_type.194, f32[1024,3072]{1,0:T(8,128)} %fusion.72, f32[3072]{0:T(1024)S(1)} %bitcast.134), kind=kOutput, calls=%fused_computation.88 | convolution fusion | flops 4865654784 | bytes 22035456 | tf_op jit(solution)/shard_map/dot_general | solution.py:150
  495.3 18.3 %reduce-scatter.5.cloned.1.call-done = f32[96,2304]{1,0:T(8,128)} async-done(((f32[768,2304]{1,0:T(8,128)}), f32[96,2304]{1,0:T(8,128)}) %reduce-scatter.5.cloned.1.call-update) | async-done | bytes 884752 | tf_op jit(solution)/shard_map/reduce_scatter | solution.py:243
  515.6 98.2 %reduce-scatter.11.cloned.1.call-done = f32[384,768]{1,0:T(8,128)} async-done(((f32[3072,768]{1,0:T(8,128)}), f32[384,768]{1,0:T(8,128)}) %reduce-scatter.11.cloned.1.call-update) | async-done | bytes 1179664 | tf_op jit(solution)/shard_map/reduce_scatter | solution.py:177
  616.0 98.1 %reduce-scatter.9.cloned.1.call-done = f32[96,3072]{1,0:T(8,128)} async-done(((f32[768,3072]{1,0:T(8,128)}), f32[96,3072]{1,0:T(8,128)}) %reduce-scatter.9.cloned.1.call-update) | async-done | bytes 1179664 | tf_op jit(solution)/shard_map/reduce_scatter | solution.py:175
  725.1 26.4 %all-reduce.17 = (bf16[768]{0:T(1024)(128)(2,1)S(1)}, bf16[768]{0:T(1024)(128)(2,1)S(1)}, bf16[768]{0:T(1024)(128)(2,1)S(1)}, bf16[768]{0:T(1024)(128)(2,1)S(1)}...) all-reduce(f32[768]{0:T(1024)S(1)} %get-tuple-element.326, ...), channel_id=2, replica_groups=mesh['rep'=4,'shard'=8] {'shard'}, use_global_device_ids=true, to_apply=%region_18.19.clone | all-reduce | flops 9216 | bytes 55296
  752.2 10.0 %all-reduce.19 = (bf16[96]{0:T(256)(128)(2,1)S(1)}, bf16[96]{0:T(256)(128)(2,1)S(1)}, bf16[96]{0:T(256)(128)(2,1)S(1)}, bf16[96]{0:T(256)(128)(2,1)S(1)}, bf16[9...) all-reduce(bf16[96]{0:T(256)(128)(2,1)S(1)} %dynamic-slice.43, ...), channel_id=1, replica_groups=mesh['rep'=4,'shard'=8] {'rep'}, use_global_device_ids=true, to_apply=%region_19.20 | all-reduce | flops 1152 | bytes 4608 | tf_op jit(solution)/shard_map/psum | solution.py:250
  (281 shorter events, 174.3 us)
Async XLA Ops:
  7.2 64.8 %all-gather.6.cloned.1.call-start = ((), (), s32[]{:S(2)}) async-start(), calls=%async_computation.4 | async-start | bytes 3981312 | tf_op jit(solution)/shard_map/all_gather | solution.py:78
  7.9 167.6 %all-gather.8.cloned.1.call-start = ((), (), s32[]{:S(2)}) async-start(), calls=%async_computation.5 | async-start | bytes 1327104 | tf_op jit(solution)/shard_map/all_gather | solution.py:81
  8.7 172.9 %all-gather.10.cloned.1.call-start = ((), (), s32[]{:S(2)}) async-start(), calls=%async_computation.6 | async-start | bytes 5308416 | tf_op jit(solution)/shard_map/all_gather | solution.py:136
  9.4 183.4 %all-gather.12.cloned.1.call-start = ((), (), s32[]{:S(2)}) async-start(), calls=%async_computation.7 | async-start | bytes 5308416 | tf_op jit(solution)/shard_map/all_gather | solution.py:138
  10.0 483.7 %reduce-scatter.7.cloned.1.call-start = ((), (), s32[]{:S(2)}) async-start(), calls=%async_computation.9 | async-start | bytes 2654208 | tf_op jit(solution)/shard_map/reduce_scatter | solution.py:246
  52.5 19.4 %copy-start.34 = (f32[768]{0:T(1024)}, f32[768]{0:T(1024)S(1)}, u32[]{:S(2)}) copy-start(f32[768]{0:T(1024)S(1)} %convert_element_type.180) | copy-start | bytes 9220
  53.1 18.8 %copy-start.50 = (f32[768]{0:T(1024)}, f32[768]{0:T(1024)S(1)}, u32[]{:S(2)}) copy-start(f32[768]{0:T(1024)S(1)} %convert_element_type.181) | copy-start | bytes 9220
  69.8 8.7 %copy-start.32 = (f32[1024]{0:T(1024)}, f32[1024]{0:T(1024)S(1)}, u32[]{:S(2)}) copy-start(f32[1024]{0:T(1024)S(1)} %broadcast_multiply_fusion.1) | copy-start | bytes 12292
  70.2 8.2 %copy-start.42 = (f32[1024]{0:T(1024)}, f32[1024]{0:T(1024)S(1)}, u32[]{:S(2)}) copy-start(f32[1024]{0:T(1024)S(1)} %fusion.53) | copy-start | bytes 12292
  70.3 8.2 %copy-start.38 = (f32[1024]{0:T(1024)}, f32[1024]{0:T(1024)S(1)}, u32[]{:S(2)}) copy-start(f32[1024]{0:T(1024)S(1)} %fusion.63) | copy-start | bytes 12292
  106.7 12.1 %copy-start.3 = (bf16[1024,12,64]{0,2,1:T(8,128)(2,1)S(1)}, bf16[1024,12,64]{0,2,1:T(8,128)(2,1)}, u32[]{:S(2)}) copy-start(bf16[1024,12,64]{0,2,1:T(8,128)(2,1)} %get-tuple-element.581) | copy-start | bytes 4718596 | tf_op jit(solution)/shard_map/while
  106.7 12.1 %copy-start.14 = (bf16[2,512,12,64]{1,3,2,0:T(8,128)(2,1)S(1)}, bf16[2,512,12,64]{1,3,2,0:T(8,128)(2,1)}, u32[]{:S(2)}) copy-start(bf16[2,512,12,64]{1,3,2,0:T(8,128)(2,1)} %get-tuple-element.564) | copy-start | bytes 4718596 | tf_op jit(solution)/shard_map/while
  146.2 12.1 %copy-start.3 = (bf16[1024,12,64]{0,2,1:T(8,128)(2,1)S(1)}, bf16[1024,12,64]{0,2,1:T(8,128)(2,1)}, u32[]{:S(2)}) copy-start(bf16[1024,12,64]{0,2,1:T(8,128)(2,1)} %get-tuple-element.581) | copy-start | bytes 4718596 | tf_op jit(solution)/shard_map/while
  146.2 12.1 %copy-start.14 = (bf16[2,512,12,64]{1,3,2,0:T(8,128)(2,1)S(1)}, bf16[2,512,12,64]{1,3,2,0:T(8,128)(2,1)}, u32[]{:S(2)}) copy-start(bf16[2,512,12,64]{1,3,2,0:T(8,128)(2,1)} %get-tuple-element.564) | copy-start | bytes 4718596 | tf_op jit(solution)/shard_map/while
  179.5 46.5 %copy-start.24 = (f32[1024]{0:T(1024)}, f32[1024]{0:T(1024)S(1)}, u32[]{:S(2)}) copy-start(f32[1024]{0:T(1024)S(1)} %broadcast_multiply_fusion) | copy-start | bytes 12292
  181.5 44.5 %copy-start.28 = (f32[1024]{0:T(1024)}, f32[1024]{0:T(1024)S(1)}, u32[]{:S(2)}) copy-start(f32[1024]{0:T(1024)S(1)} %fusion.64) | copy-start | bytes 12292
  181.5 11.3 %copy-start.36 = (f32[1024]{0:T(1024)S(1)}, f32[1024]{0:T(1024)}, u32[]{:S(2)}) copy-start(f32[1024]{0:T(1024)} %convert_element_type.197) | copy-start | bytes 12292
  181.5 11.3 %copy-start.47 = (f32[8,1,384]{2,1,0:T(1,128)S(1)}, f32[8,1,384]{2,1,0:T(1,128)}, u32[]{:S(2)}) copy-start(f32[8,1,384]{2,1,0:T(1,128)} %convert_element_type.233) | copy-start | bytes 36868
  192.8 17.7 %copy-start.19 = (bf16[768,3072]{1,0:T(8,128)(2,1)S(1)}, bf16[768,3072]{1,0:T(8,128)(2,1)}, u32[]{:S(2)}) copy-start(bf16[768,3072]{1,0:T(8,128)(2,1)} %all-gather.10.cloned.1.call-done) | copy-start | bytes 14155780
  210.5 7.4 copy-start.55
  221.4 4.7 copy-start.10
  246.6 267.0 %reduce-scatter.5.cloned.1.call-start = ((), (), s32[]{:S(2)}) async-start(), calls=%async_computation.8 | async-start | bytes 7962624 | tf_op jit(solution)/shard_map/reduce_scatter | solution.py:243
  252.1 11.6 %copy-start.11 = (bf16[2,512,12,64]{1,3,2,0:T(8,128)(2,1)S(1)}, bf16[2,512,12,64]{1,3,2,0:T(8,128)(2,1)}, u32[]{:S(2)}) copy-start(bf16[2,512,12,64]{1,3,2,0:T(8,128)(2,1)} %get-tuple-element.622) | copy-start | bytes 4718596 | tf_op jit(solution)/shard_map/while
  316.2 9.5 %copy-start.2 = (bf16[2,512,12,64]{1,3,2,0:T(8,128)(2,1)S(1)}, bf16[2,512,12,64]{1,3,2,0:T(8,128)(2,1)}, u32[]{:S(2)}) copy-start(bf16[2,512,12,64]{1,3,2,0:T(8,128)(2,1)} %copy-done.1) | copy-start | bytes 4718596 | tf_op jit(solution)/shard_map/while
  338.3 11.4 %copy-start.11 = (bf16[2,512,12,64]{1,3,2,0:T(8,128)(2,1)S(1)}, bf16[2,512,12,64]{1,3,2,0:T(8,128)(2,1)}, u32[]{:S(2)}) copy-start(bf16[2,512,12,64]{1,3,2,0:T(8,128)(2,1)} %get-tuple-element.622) | copy-start | bytes 4718596 | tf_op jit(solution)/shard_map/while
  402.7 9.5 %copy-start.2 = (bf16[2,512,12,64]{1,3,2,0:T(8,128)(2,1)S(1)}, bf16[2,512,12,64]{1,3,2,0:T(8,128)(2,1)}, u32[]{:S(2)}) copy-start(bf16[2,512,12,64]{1,3,2,0:T(8,128)(2,1)} %copy-done.1) | copy-start | bytes 4718596 | tf_op jit(solution)/shard_map/while
  437.3 176.5 %reduce-scatter.11.cloned.1.call-start = ((), (), s32[]{:S(2)}) async-start(), calls=%async_computation.11 | async-start | bytes 10616832 | tf_op jit(solution)/shard_map/reduce_scatter | solution.py:177
  452.7 261.4 %reduce-scatter.9.cloned.1.call-start = ((), (), s32[]{:S(2)}) async-start(), calls=%async_computation.10 | async-start | bytes 10616832 | tf_op jit(solution)/shard_map/reduce_scatter | solution.py:175
  464.3 317.5 %all-reduce.23.cloned.1.call-start = ((), (), s32[]{:S(2)}) async-start(), calls=%async_computation.12 | async-start | bytes 3538944 | tf_op jit(solution)/shard_map/psum | solution.py:252
  716.2 5.1 copy-start.43
  721.2 45.7 %copy-start.41 = (f32[1024]{0:T(1024)S(1)}, f32[1024]{0:T(1024)}, u32[]{:S(2)}) copy-start(f32[1024]{0:T(1024)} %copy-done.40) | copy-start | bytes 12292
  781.8 5.9 copy-start.23
  (39 other events, 101.5 us)
Sparse Core Ops, SparseCore 0:
  9.7 44.9 all-gather.5
  56.3 21.4 all-gather.7
  79.4 51.4 all-gather.9
  132.4 50.5 all-gather.11
  246.7 35.0 reduce-scatter.6
  437.4 76.1 reduce-scatter.4
  515.9 97.8 reduce-scatter.10
  616.1 97.8 reduce-scatter.8
  718.6 63.1 all-reduce.22
where the time goes:
time: 803 us; the launch traced here: 795 us
  matrix products  275 us (34%)
  waiting for transfers between devices  224 us (28%)
  other arithmetic  121 us (15%)
  blocking collectives  80.8 us (10%)
  local copies, waits for them, and re-layouts  69.8 us (9%)
  between operations  16.7 us (2%)
  loops' own time  8.67 us (1%)
    reduce_scatter x1, waiting for transfers between devices, local(): lax.psum_scatter(grad_proj, 'shard', scatter_dimension=0, tiled=True)  98.2 us
    reduce_scatter x1, waiting for transfers between devices, local(): lax.psum_scatter(grad_fc, 'shard', scatter_dimension=0, tiled=True)  98.1 us
    unnamed x2, blocking collectives  58.1 us
    dot_general x4, matrix products, block_scores(): jnp.einsum('qhd,khd->hqk', query_rows, keys_all, preferred_element_type=j...  44.9 us
    convert_element_type x2, other arithmetic, backward_block(): back_scores = (weights_f * (back_weights - inner_sum)).astype(jnp.bfloat16)  42.3 us
    dot_general x4, matrix products, times_transposed(): lax.dot_general(left, right, (((1,), (1,)), ((), ())), preferred_element_...  38.4 us
    dot_general x2, matrix products, backward_block(): jnp.einsum('qhd,khd->hqk', upstream_rows, values_all, preferred_element_t...  36.4 us
    dot_general x4, matrix products, contract_rows(): lax.dot_general(left, right, (((0,), (0,)), ((), ())), preferred_element_...  34.7 us
  transfers between devices with their start and end apart: 9, of which 4 were waited for; matrix products, arithmetic and copies ran while one was open for 50% of the time, Pallas kernels for 0%

commit v1 on v0

v1 whole, which is shorter than its diff:
```python
import functools

import jax
import jax.numpy as jnp
from jax import lax
from jax.experimental import pallas as pl
from jax.experimental.pallas import tpu as pltpu
from jax.sharding import PartitionSpec as P

HEADS = 12
HEAD_DIM = 64
BLOCK = 128
PAIR = 2 * HEAD_DIM
ROWS = 256
MASKED = -1e30
MIB = 1 << 20
F32 = jnp.float32
BF16 = jnp.bfloat16


def dot(left, right):
    return lax.dot_general(left, right, (((1,), (0,)), ((), ())), preferred_element_type=F32)


def dot_nt(left, right):
    return lax.dot_general(left, right, (((1,), (1,)), ((), ())), preferred_element_type=F32)


def dot_tn(left, right):
    return lax.dot_general(left, right, (((0,), (0,)), ((), ())), preferred_element_type=F32)


def normalise(values):
    average = jnp.mean(values, axis=-1, keepdims=True)
    centred = values - average
    variance = jnp.mean(centred * centred, axis=-1, keepdims=True)
    scale = lax.rsqrt(variance + 1e-05)
    return centred * scale, scale


def normalise_back(back_hat, hat, scale):
    inner = jnp.mean(back_hat * hat, axis=-1, keepdims=True)
    return scale * (back_hat - jnp.mean(back_hat, axis=-1, keepdims=True) - hat * inner)


def live_rows(lengths_ref, blocks_ref, first_row, shape):
    rows = first_row + lax.broadcasted_iota(jnp.int32, shape, 0)
    live = None
    for slot in range(lengths_ref.shape[0]):
        start = blocks_ref[slot] * BLOCK
        inside = (rows >= start) & (rows < start + lengths_ref[slot])
        live = inside if live is None else live | inside
    return live


def const_spec(shape):
    return pl.BlockSpec(shape, lambda *_: (0,) * len(shape), pipeline_mode=pl.Buffered(1))


def smem_spec():
    return pl.BlockSpec(memory_space=pltpu.SMEM)


def params(mib):
    return pltpu.CompilerParams(vmem_limit_bytes=mib * MIB, dimension_semantics=("arbitrary",))


def qkv_kernel(x_ref, gain_ref, bias_ref, shift_ref, w_ref, h_ref, qkv_ref):
    hat, _ = normalise(x_ref[...].astype(F32))
    h_one = (hat * gain_ref[...] + bias_ref[...]).astype(BF16)
    h_ref[...] = h_one
    width = x_ref.shape[1]
    for part in range(3):
        cols = slice(part * width, (part + 1) * width)
        out = (dot(h_one, w_ref[:, cols]) + shift_ref[:, cols]).astype(BF16)
        if part == 0:
            out = out * BF16(HEAD_DIM**-0.5)
        qkv_ref[:, cols] = out


def project_qkv(x, gain, bias, shift, w):
    rows, width = x.shape
    wide = w.shape[1]
    return pl.pallas_call(
        qkv_kernel,
        grid=(rows // ROWS,),
        in_specs=[
            pl.BlockSpec((ROWS, width), lambda i: (i, 0)),
            const_spec((1, width)),
            const_spec((1, width)),
            const_spec((1, wide)),
            const_spec((width, wide)),
        ],
        out_specs=[
            pl.BlockSpec((ROWS, width), lambda i: (i, 0)),
            pl.BlockSpec((ROWS, wide), lambda i: (i, 0)),
        ],
        out_shape=[
            jax.ShapeDtypeStruct((rows, width), BF16),
            jax.ShapeDtypeStruct((rows, wide), BF16),
        ],
        compiler_params=params(40),
        cost_estimate=pl.CostEstimate(
            flops=2 * rows * width * wide, bytes_accessed=2 * width * wide + 10 * rows * width, transcendentals=rows
        ),
        name="ln1_qkv",
    )(x, gain, bias, shift, w)


def segment_lanes(lengths_ref, blocks_ref, penalty_ref, member_ref):
    rows = penalty_ref.shape[0]
    shape = (rows, PAIR)
    first = lax.broadcasted_iota(jnp.int32, shape, 0) & ~(BLOCK - 1)
    lane = lax.broadcasted_iota(jnp.int32, shape, 1) & (HEAD_DIM - 1)
    slots = lengths_ref.shape[0]
    member = jnp.full(shape, slots, jnp.int32)
    for slot in range(slots):
        start = blocks_ref[slot] * BLOCK
        inside = (first >= start) & (first < start + lengths_ref[slot])
        member = jnp.where(inside, slot, member)
    same = member == lane
    member_ref[...] = jnp.where(same, 1.0, 0.0).astype(BF16)
    penalty_ref[...] = jnp.where(same | (lane > slots), 0.0, MASKED).astype(BF16)


def low_lanes(rows):
    return lax.broadcasted_iota(jnp.int32, (rows, PAIR), 1) < HEAD_DIM


def attend_kernel(
    lengths_ref, blocks_ref, q_ref, k_ref, v_ref, out_ref, log_ref, penalty_ref, member_ref, key_ref, value_ref
):
    rows = q_ref.shape[0]

    @pl.when(pl.program_id(0) == 0)
    def _():
        segment_lanes(lengths_ref, blocks_ref, penalty_ref, member_ref)

    low = low_lanes(rows)
    one = jnp.ones((), BF16)
    key_ref[0] = jnp.where(low, k_ref[...], member_ref[...])
    key_ref[1] = jnp.where(low, member_ref[...], k_ref[...])
    value_ref[0] = jnp.where(low, v_ref[...], one)
    value_ref[1] = jnp.where(low, one, v_ref[...])
    low = low_lanes(ROWS)
    causal = lax.broadcasted_iota(jnp.int32, (ROWS, ROWS), 1) <= lax.broadcasted_iota(jnp.int32, (ROWS, ROWS), 0)
    for block in range(rows // ROWS):
        here = slice(block * ROWS, (block + 1) * ROWS)
        before = slice(0, block * ROWS)
        q, penalty = q_ref[here], penalty_ref[here]
        mixed, logs = [], []
        for head in range(2):
            q_head = jnp.where(low, q, penalty) if head == 0 else jnp.where(low, penalty, q)
            near = jnp.where(causal, dot_nt(q_head, key_ref[head, here]), MASKED)
            largest = jnp.max(near, axis=-1, keepdims=True)
            if block:
                far = dot_nt(q_head, key_ref[head, before])
                largest = jnp.maximum(largest, jnp.max(far, axis=-1, keepdims=True))
            total = dot(jnp.exp(near - largest).astype(BF16), value_ref[head, here])
            if block:
                total = total + dot(jnp.exp(far - largest).astype(BF16), value_ref[head, before])
            weight = pltpu.roll(total, HEAD_DIM, 1)
            mixed.append(total / weight)
            logs.append(largest + jnp.log(weight))
        out = jnp.where(low, mixed[0], mixed[1]).astype(BF16)
        live = live_rows(lengths_ref, blocks_ref, block * ROWS, (ROWS, PAIR))
        out_ref[here] = jnp.where(live, out, v_ref[here])
        turned = jnp.where(low, logs[0], logs[1]).T
        log_ref[0, 0:1, here] = turned[0:1]
        log_ref[0, 1:2, here] = turned[HEAD_DIM : HEAD_DIM + 1]


def attend(lengths, blocks, qkv):
    rows = qkv.shape[0]
    width = qkv.shape[1] // 3
    pairs = width // PAIR
    return pl.pallas_call(
        attend_kernel,
        grid=(pairs,),
        in_specs=[
            smem_spec(),
            smem_spec(),
            pl.BlockSpec((rows, PAIR), lambda i: (0, i)),
            pl.BlockSpec((rows, PAIR), lambda i: (0, pairs + i)),
            pl.BlockSpec((rows, PAIR), lambda i: (0, 2 * pairs + i)),
        ],
        out_specs=[
            pl.BlockSpec((rows, PAIR), lambda i: (0, i)),
            pl.BlockSpec((1, 2, rows), lambda i: (i, 0, 0)),
        ],
        out_shape=[
            jax.ShapeDtypeStruct((rows, width), BF16),
            jax.ShapeDtypeStruct((pairs, 2, rows), F32),
        ],
        scratch_shapes=[
            pltpu.VMEM((rows, PAIR), BF16),
            pltpu.VMEM((rows, PAIR), BF16),
            pltpu.VMEM((2, rows, PAIR), BF16),
            pltpu.VMEM((2, rows, PAIR), BF16),
        ],
        compiler_params=params(40),
        cost_estimate=pl.CostEstimate(
            flops=8 * rows * rows * width, bytes_accessed=8 * rows * width, transcendentals=rows * rows * pairs
        ),
        name="attend",
    )(lengths, blocks, qkv, qkv, qkv)


def attend_back_kernel(
    lengths_ref,
    blocks_ref,
    q_ref,
    k_ref,
    v_ref,
    out_ref,
    back_ref,
    log_ref,
    grad_ref,
    sums_ref,
    penalty_ref,
    member_ref,
    q_seg,
    q_own,
    back_own,
    q_grad,
):
    rows = q_ref.shape[0]

    @pl.when(pl.program_id(0) == 0)
    def _():
        segment_lanes(lengths_ref, blocks_ref, penalty_ref, member_ref)

    low = low_lanes(rows)
    zero = jnp.zeros((), BF16)
    q, back, penalty = q_ref[...], back_ref[...], penalty_ref[...]
    q_seg[0] = jnp.where(low, q, penalty)
    q_seg[1] = jnp.where(low, penalty, q)
    q_own[0] = jnp.where(low, q, zero)
    q_own[1] = jnp.where(low, zero, q)
    back_own[0] = jnp.where(low, back, zero)
    back_own[1] = jnp.where(low, zero, back)
    inner = (back.astype(F32) * out_ref[...].astype(F32)).T
    inner = [jnp.sum(inner[:HEAD_DIM], axis=0, keepdims=True), jnp.sum(inner[HEAD_DIM:], axis=0, keepdims=True)]
    q_grad[...] = jnp.zeros_like(q_grad)
    low = low_lanes(ROWS)
    causal = lax.broadcasted_iota(jnp.int32, (ROWS, ROWS), 0) <= lax.broadcasted_iota(jnp.int32, (ROWS, ROWS), 1)
    value_sum = jnp.zeros((1, PAIR), F32)
    for block in range(rows // ROWS):
        here = slice(block * ROWS, (block + 1) * ROWS)
        after = slice((block + 1) * ROWS, rows)
        k, v, member = k_ref[here], v_ref[here], member_ref[here]
        key_grad = jnp.zeros((ROWS, PAIR), F32)
        value_grad = jnp.zeros((ROWS, PAIR), F32)
        for head in range(2):
            pick = (lambda a, b: jnp.where(low, a, b)) if head == 0 else (lambda a, b: jnp.where(low, b, a))
            k_seg, k_own, v_own = pick(k, member), pick(k, zero), pick(v, zero)
            for cols in (here, after):
                if cols.start == cols.stop:
                    continue
                prob = jnp.exp(dot_nt(k_seg, q_seg[head, cols]) - log_ref[0, head : head + 1, cols])
                if cols is here:
                    prob = jnp.where(causal, prob, 0.0)
                back_prob = dot_nt(v_own, back_ref[cols])
                back_scores = (prob * (back_prob - inner[head][:, cols])).astype(BF16)
                value_grad = value_grad + dot(prob.astype(BF16), back_own[head, cols])
                key_grad = key_grad + dot(back_scores, q_own[head, cols])
                q_grad[cols] += dot_tn(back_scores, k_own)
        key_low, value_low = key_grad.astype(BF16), value_grad.astype(BF16)
        grad_ref[1, here] = key_low
        grad_ref[2, here] = value_low
        value_sum = value_sum + jnp.sum(value_low.astype(F32), axis=0, keepdims=True)
    q_low = (q_grad[...] * (HEAD_DIM**-0.5)).astype(BF16)
    grad_ref[0] = q_low
    sums_ref[0, 0:1] = jnp.sum(q_low.astype(F32), axis=0, keepdims=True)
    sums_ref[0, 1:2] = value_sum


def attend_back(lengths, blocks, qkv, attn, back_attn, logs):
    rows, width = attn.shape
    pairs = width // PAIR
    own = pl.BlockSpec((rows, PAIR), lambda i: (0, i))
    return pl.pallas_call(
        attend_back_kernel,
        grid=(pairs,),
        in_specs=[
            smem_spec(),
            smem_spec(),
            own,
            pl.BlockSpec((rows, PAIR), lambda i: (0, pairs + i)),
            pl.BlockSpec((rows, PAIR), lambda i: (0, 2 * pairs + i)),
            own,
            own,
            pl.BlockSpec((1, 2, rows), lambda i: (i, 0, 0)),
        ],
        out_specs=[
            pl.BlockSpec((3, rows, PAIR), lambda i: (0, 0, i)),
            pl.BlockSpec((1, 2, PAIR), lambda i: (i, 0, 0)),
        ],
        out_shape=[
            jax.ShapeDtypeStruct((3, rows, width), BF16),
            jax.ShapeDtypeStruct((pairs, 2, PAIR), F32),
        ],
        scratch_shapes=[
            pltpu.VMEM((rows, PAIR), BF16),
            pltpu.VMEM((rows, PAIR), BF16),
            pltpu.VMEM((2, rows, PAIR), BF16),
            pltpu.VMEM((2, rows, PAIR), BF16),
            pltpu.VMEM((2, rows, PAIR), BF16),
            pltpu.VMEM((rows, PAIR), F32),
        ],
        compiler_params=params(48),
        cost_estimate=pl.CostEstimate(
            flops=20 * rows * rows * width, bytes_accessed=16 * rows * width, transcendentals=rows * rows * pairs
        ),
        name="attend_back",
    )(lengths, blocks, qkv, qkv, qkv, attn, back_attn, logs)


def mlp_kernel(
    lengths_ref,
    blocks_ref,
    x_ref,
    attn_ref,
    cot_ref,
    out_bias_ref,
    gain_ref,
    bias_ref,
    fc_bias_ref,
    proj_bias_ref,
    w_out_ref,
    w_fc_ref,
    w_proj_ref,
    output_ref,
    h_ref,
    act_ref,
    back_mlp_ref,
    back_pre_ref,
    back_resid_ref,
    back_branch_ref,
    back_attn_ref,
    sums_ref,
    fc_sums_ref,
):
    step = pl.program_id(0)
    rows, width = x_ref.shape
    hidden = w_fc_ref.shape[1]

    @pl.when(step == 0)
    def _():
        sums_ref[...] = jnp.zeros_like(sums_ref)
        fc_sums_ref[...] = jnp.zeros_like(fc_sums_ref)

    resid = x_ref[...].astype(F32) + dot(attn_ref[...], w_out_ref[...]) + out_bias_ref[...]
    hat, scale = normalise(resid)
    gain = gain_ref[...]
    h_two = (hat * gain + bias_ref[...]).astype(BF16)
    h_ref[...] = h_two
    live = live_rows(lengths_ref, blocks_ref, step * rows, (rows, width))
    back_mlp = jnp.where(live, cot_ref[...], jnp.zeros((), BF16))
    back_mlp_ref[...] = back_mlp
    upstream = back_mlp.astype(F32)
    mlp = jnp.zeros((rows, width), F32)
    back_h = jnp.zeros((rows, width), F32)
    for first in range(0, hidden, width):
        cols = slice(first, first + width)
        pre = dot(h_two, w_fc_ref[:, cols]) + fc_bias_ref[:, cols]
        square = pre * pre
        bent = jnp.tanh(0.7978845608028654 * (pre + 0.044715 * (square * pre)))
        half = 0.5 * (1.0 + bent)
        act = (pre * half).astype(BF16)
        act_ref[:, cols] = act
        slope = half + 0.5 * pre * (1.0 - bent * bent) * (0.7978845608028654 + 0.1070322242 * square)
        mlp = mlp + dot(act, w_proj_ref[cols])
        back_pre = (dot_nt(back_mlp, w_proj_ref[cols]) * slope).astype(BF16)
        back_pre_ref[:, cols] = back_pre
        fc_sums_ref[:, cols] += jnp.sum(back_pre.astype(F32), axis=0, keepdims=True)
        back_h = back_h + dot_nt(back_pre, w_fc_ref[:, cols])
    output_ref[...] = (resid + mlp + proj_bias_ref[...]).astype(BF16)
    back_resid = upstream + normalise_back(back_h * gain, hat, scale)
    back_resid_ref[...] = back_resid
    back_branch = back_resid.astype(BF16)
    back_branch_ref[...] = back_branch
    back_attn_ref[...] = dot_nt(back_branch, w_out_ref[...]).astype(BF16)
    sums_ref[0:1] += jnp.sum(back_h * hat, axis=0, keepdims=True)
    sums_ref[1:2] += jnp.sum(back_h, axis=0, keepdims=True)
    sums_ref[2:3] += jnp.sum(upstream, axis=0, keepdims=True)
    sums_ref[3:4] += jnp.sum(back_branch.astype(F32), axis=0, keepdims=True)


def mlp_both_ways(lengths, blocks, x, attn, cot, out_bias, gain, bias, fc_bias, proj_bias, w_out, w_fc, w_proj):
    rows, width = x.shape
    hidden = w_fc.shape[1]
    tile = pl.BlockSpec((ROWS, width), lambda i: (i, 0))
    wide = pl.BlockSpec((ROWS, hidden), lambda i: (i, 0))
    vec = const_spec((1, width))

    def shaped(cols, kind):
        return jax.ShapeDtypeStruct((rows, cols), kind)

    return pl.pallas_call(
        mlp_kernel,
        grid=(rows // ROWS,),
        in_specs=[smem_spec(), smem_spec(), tile, tile, tile, vec, vec, vec, const_spec((1, hidden)), vec]
        + [const_spec(w_out.shape), const_spec(w_fc.shape), const_spec(w_proj.shape)],
        out_specs=[tile, tile, wide, tile, wide, tile, tile, tile]
        + [pl.BlockSpec((8, width), lambda i: (0, 0)), pl.BlockSpec((1, hidden), lambda i: (0, 0))],
        out_shape=[
            shaped(width, BF16),
            shaped(width, BF16),
            shaped(hidden, BF16),
            shaped(width, BF16),
            shaped(hidden, BF16),
            shaped(width, F32),
            shaped(width, BF16),
            shaped(width, BF16),
            jax.ShapeDtypeStruct((8, width), F32),
            jax.ShapeDtypeStruct((1, hidden), F32),
        ],
        compiler_params=params(58),
        cost_estimate=pl.CostEstimate(
            flops=4 * rows * width * (width + 2 * hidden),
            bytes_accessed=40 * rows * width,
            transcendentals=rows * hidden,
        ),
        name="mlp",
    )(lengths, blocks, x, attn, cot, out_bias, gain, bias, fc_bias, proj_bias, w_out, w_fc, w_proj)


def tn_kernel(left_ref, right_ref, out_ref):
    out_ref[...] = dot_tn(left_ref[...], right_ref[...].reshape(left_ref.shape[0], -1)).astype(out_ref.dtype)


def weight_grad(left, right, by_left, name):
    rows = left.shape[0]
    unit = 768
    if right.ndim == 3:
        steps, right_spec = right.shape[0], pl.BlockSpec((1, rows, unit), lambda i: (i, 0, 0))
        shape = (left.shape[1], right.shape[0] * unit)
    else:
        steps = max(left.shape[1], right.shape[1]) // unit
        right_spec = pl.BlockSpec((rows, unit), lambda i: (0, 0 if by_left else i))
        shape = (left.shape[1], right.shape[1])
    return pl.pallas_call(
        tn_kernel,
        grid=(steps,),
        in_specs=[pl.BlockSpec((rows, unit), lambda i: (0, i if by_left else 0)), right_spec],
        out_specs=pl.BlockSpec((unit, unit), lambda i: (i, 0) if by_left else (0, i)),
        out_shape=jax.ShapeDtypeStruct(shape, BF16),
        compiler_params=params(40),
        cost_estimate=pl.CostEstimate(
            flops=2 * rows * shape[0] * shape[1], bytes_accessed=2 * shape[0] * shape[1], transcendentals=0
        ),
        name=name,
    )(left, right)


def qkv_back_kernel(x_ref, gain_ref, w_ref, back_ref, resid_ref, out_ref, sums_ref):
    @pl.when(pl.program_id(0) == 0)
    def _():
        sums_ref[...] = jnp.zeros_like(sums_ref)

    width = x_ref.shape[1]
    back_h = dot_nt(back_ref[0], w_ref[:, :width])
    back_h = back_h + dot_nt(back_ref[1], w_ref[:, width : 2 * width])
    back_h = back_h + dot_nt(back_ref[2], w_ref[:, 2 * width :])
    hat, scale = normalise(x_ref[...].astype(F32))
    out_ref[...] = (resid_ref[...] + normalise_back(back_h * gain_ref[...], hat, scale)).astype(BF16)
    sums_ref[0:1] += jnp.sum(back_h * hat, axis=0, keepdims=True)
    sums_ref[1:2] += jnp.sum(back_h, axis=0, keepdims=True)


def qkv_back(x, gain, w, back_qkv, back_resid):
    rows, width = x.shape
    tile = pl.BlockSpec((ROWS, width), lambda i: (i, 0))
    return pl.pallas_call(
        qkv_back_kernel,
        grid=(rows // ROWS,),
        in_specs=[
            tile,
            const_spec((1, width)),
            const_spec(w.shape),
            pl.BlockSpec((3, ROWS, width), lambda i: (0, i, 0)),
            tile,
        ],
        out_specs=[tile, pl.BlockSpec((8, width), lambda i: (0, 0))],
        out_shape=[jax.ShapeDtypeStruct((rows, width), BF16), jax.ShapeDtypeStruct((8, width), F32)],
        compiler_params=params(40),
        cost_estimate=pl.CostEstimate(
            flops=6 * rows * width * width, bytes_accessed=20 * rows * width, transcendentals=rows
        ),
        name="qkv_back",
    )(x, gain, w, back_qkv, back_resid)


def gather(value):
    return lax.all_gather(value, "shard", axis=0, tiled=True)


def spread(value):
    own = lax.psum_scatter(value.astype(BF16), "shard", scatter_dimension=0, tiled=True)
    return lax.psum(own, "rep").astype(F32)


def local(
    tokens,
    cotangent,
    seq_lengths,
    seq_blocks,
    ln1_gain,
    ln1_bias,
    w_qkv,
    q_bias,
    v_bias,
    w_out,
    out_bias,
    ln2_gain,
    ln2_bias,
    w_fc,
    fc_bias,
    w_proj,
    proj_bias,
):
    width = tokens.shape[1]
    small = jnp.concatenate(
        [ln1_gain, ln1_bias, q_bias, v_bias, out_bias, ln2_gain, ln2_bias, proj_bias, fc_bias]
    ).reshape(1, -1)
    own = w_qkv.shape[0]
    small = gather(small).astype(F32)

    def vec(index, count=1):
        return small[:, index * own : (index + count) * own].reshape(1, -1)

    gain_one, bias_one, query_shift, value_shift, out_shift, gain_two, bias_two, proj_shift = (
        vec(index) for index in range(8)
    )
    fc_shift = vec(8, fc_bias.shape[0] // own)
    qkv_shift = jnp.concatenate([query_shift, jnp.zeros_like(query_shift), value_shift], axis=1)
    full_qkv, full_out, full_fc, full_proj = gather(w_qkv), gather(w_out), gather(w_fc), gather(w_proj)
    h_one, qkv = project_qkv(tokens, gain_one, bias_one, qkv_shift, full_qkv)
    attn, logs = attend(seq_lengths, seq_blocks, qkv)
    output, h_two, act, back_mlp, back_pre, back_resid, back_branch, back_attn, mlp_sums, fc_sums = mlp_both_ways(
        seq_lengths,
        seq_blocks,
        tokens,
        attn,
        cotangent,
        out_shift,
        gain_two,
        bias_two,
        fc_shift,
        proj_shift,
        full_out,
        full_fc,
        full_proj,
    )
    grad_proj = weight_grad(act, back_mlp, True, "grad_proj")
    grad_fc = weight_grad(h_two, back_pre, False, "grad_fc")
    grad_out = weight_grad(attn, back_branch, False, "grad_out")
    back_qkv, qkv_sums = attend_back(seq_lengths, seq_blocks, qkv, attn, back_attn, logs)
    grad_qkv = weight_grad(h_one, back_qkv, False, "grad_qkv")
    token_grad, ln_sums = qkv_back(tokens, gain_one, full_qkv, back_qkv, back_resid)
    return (
        output,
        token_grad,
        spread(ln_sums[0]),
        spread(ln_sums[1]),
        spread(grad_qkv),
        spread(qkv_sums[:, 0].reshape(-1)),
        spread(qkv_sums[:, 1].reshape(-1)),
        spread(grad_out),
        spread(mlp_sums[3]),
        spread(mlp_sums[0]),
        spread(mlp_sums[1]),
        spread(grad_fc),
        spread(fc_sums[0]),
        spread(grad_proj),
        spread(mlp_sums[2]),
    )


def solution(mesh):
    both = ("rep", "shard")
    matrix, vector = P("shard", None), P("shard")
    return jax.shard_map(
        local,
        mesh=mesh,
        in_specs=(
            P(both, None),
            P(both, None),
            P(both),
            P(both),
            vector,
            vector,
            matrix,
            vector,
            vector,
            matrix,
            vector,
            vector,
            vector,
            matrix,
            vector,
            matrix,
            vector,
        ),
        out_specs=(
            P(both, None),
            P(both, None),
            vector,
            vector,
            matrix,
            vector,
            vector,
            matrix,
            vector,
            vector,
            vector,
            matrix,
            vector,
            matrix,
            vector,
        ),
        check_vma=False,
    )
```

time: 803 us -> 499 us (0.62)
  matrix products: 275 us -> 0 us
  Pallas kernels: 0 us -> 126 us
  other arithmetic: 121 us -> 9.8 us
  waiting for transfers between devices: 224 us -> 261 us
  local copies, waits for them, and re-layouts: 69.8 us -> 34 us
  blocking collectives: 80.8 us -> 51.7 us
  loops' own time: 8.67 us -> 0 us
    dot_general x26 -> x0, matrix products: 275 us -> none  [the longest x4 44.9 us: block_scores(): jnp.einsum('qhd,khd->hqk', query_rows, keys_all, preferred_element_type=j...]
    pallas_call x0 -> x9, Pallas kernels: none -> 126 us  [the longest x1 35.5 us: mlp_both_ways(): pl.pallas_call(mlp_kernel, grid=(rows // ROWS,), in_specs=[smem_spec(), s...]
    all_gather x4, waiting for transfers between devices: 0.04 us -> 118 us  [gather(): return lax.all_gather(value, 'shard', axis=0, tiled=True)]
    reduce_scatter x4, waiting for transfers between devices: 215 us -> 129 us  [spread(): lax.psum_scatter(value.astype(BF16), 'shard', scatter_dimension=0, tiled=...]
    convert_element_type x30 -> x14, other arithmetic: 70.8 us -> 9.78 us  [the longest x13 9.74 us: spread(): return lax.psum(own, 'rep').astype(F32)]
    reduce_sum x12 -> x0, other arithmetic: 41.1 us -> none  [the longest x2 24.2 us: forward_block(): totals = jnp.sum(jnp.exp(scores - largest), axis=-1, keepdims=True)]
    unnamed x2 -> x1, blocking collectives: 58.1 us -> 26 us
    another operation x4 -> x0, local copies, waits for them, and re-layouts: 9.7 us -> none
  transfers between devices with their start and end apart: 9 -> 9, of which waited for: 4 -> 7; matrix products, arithmetic and copies ran while one was open for 50% -> 2% of each run, Pallas kernels for 0% -> 18%
where the time goes in v1:
time: 499 us; the launch traced here: 498 us
  waiting for transfers between devices  261 us (52%)
  Pallas kernels  126 us (25%)
  blocking collectives  51.7 us (10%)
  local copies, waits for them, and re-layouts  34 us (7%)
  between operations  15.5 us (3%)
  other arithmetic  9.8 us (2%)
    reduce_scatter x4, waiting for transfers between devices, spread(): lax.psum_scatter(value.astype(BF16), 'shard', scatter_dimension=0, tiled=...  129 us
    all_gather x4, waiting for transfers between devices, gather(): return lax.all_gather(value, 'shard', axis=0, tiled=True)  118 us
    pallas_call x1, Pallas kernels, mlp_both_ways(): pl.pallas_call(mlp_kernel, grid=(rows // ROWS,), in_specs=[smem_spec(), s...  35.5 us
    pallas_call x1, Pallas kernels, attend_back(): pl.pallas_call(attend_back_kernel, grid=(pairs,), in_specs=[smem_spec(),...  33.6 us
    unnamed x88, local copies, waits for them, and re-layouts  30.8 us
    unnamed x1, blocking collectives  26 us
    pallas_call x1, Pallas kernels, attend(): pl.pallas_call(attend_kernel, grid=(pairs,), in_specs=[smem_spec(), smem_...  24.2 us
    pallas_call x4, Pallas kernels, weight_grad(): pl.pallas_call(tn_kernel, grid=(steps,), in_specs=[pl.BlockSpec((rows, un...  20.5 us
  transfers between devices with their start and end apart: 9, of which 7 were waited for; matrix products, arithmetic and copies ran while one was open for 2% of the time, Pallas kernels for 18%

profile of v1, /device:TPU:0, one launch (start us, length us, event | category | flops | bytes accessed | tf_op | source)
XLA Modules:
  0.0 498.0 jit_solution(3922526913985789518)
XLA Ops:
  10.3 15.8 %all-gather.1 = bf16[8,1,1152]{2,1,0:T(2,128)(2,1)S(1)} all-gather(bf16[1,1,1152]{2,1,0:T(2,128)(2,1)S(1)} %reshape.81), channel_id=2, replica_groups=mesh['rep'=4,'shard'=8] {'shard'}, dimensions={0}, use_global_device_ids=true | all-gather | bytes 20736 | tf_op jit(solution)/shard_map/all_gather | solution.py:496
  29.8 24.2 %all-gather.7.cloned.1.call-done.w_ref = bf16[768,2304]{1,0:T(8,128)(2,1)} async-done(((bf16[96,2304]{1,0:T(8,128)(2,1)}), bf16[768,2304]{1,0:T(8,128)(2,1)}) %all-gather.7.cloned.1.call-update) | async-done | bytes 3538960 | tf_op jit(solution)/shard_map/all_gather | solution.py:496
  54.1 2.0 copy-done.2
  56.1 5.2 %ln1_qkv.1 = (bf16[1024,768]{1,0:T(8,128)(2,1)S(1)}, bf16[1024,2304]{1,0:T(8,128)(2,1)S(1)}) custom-call(bf16[1024,768]{1,0:T(8,128)(2,1)S(1)} %copy-done.4, f32[1,768]{1,0:T(1,128)S(1)} %reshape.70.gain_ref, f32[1,768]{1,0:T(1,128)S(1)} %reshape.71.bias_ref, f32[1,2304]{1,0:T(1,128)S(1)} %fusion.shift_ref, bf16[768,2304]{1,0:T(8,128)(2,1)S(1)} %copy-done.2), custom_call_target="tpu_custom_call" | custom-call | flops 3623878656 | bytes 11403264 | tf_op jit(solution)/shard_map/ln1_qkv/pallas_call | solution.py:84
  61.3 24.2 %attend.1 = (bf16[1024,768]{1,0:T(8,128)(2,1)S(1)}, f32[6,2,1024]{2,1,0:T(2,128)S(1)}) custom-call(s32[4]{0:T(128)S(1)} %copy-done.6, s32[4]{0:T(128)S(1)} %copy-done.8, bf16[1024,2304]{1,0:T(8,128)(2,1)S(1)} %get-tuple-element.33.q_ref.k_ref.v_ref, bf16[1024,2304]{1,0:T(8,128)(2,1)S(1)} %get-tuple-element.33.q_ref.k_ref.v_ref, ...), custom_call_target="tpu_custom_call" | custom-call | flops 6442450944 | bytes 6291456 | tf_op jit(solution)/shard_map/attend/pallas_call | solution.py:177
  86.7 2.2 copy-done.18
  88.9 41.6 %all-gather.11.cloned.1.call-done.w_fc_ref = bf16[768,3072]{1,0:T(8,128)(2,1)} async-done(((bf16[96,3072]{1,0:T(8,128)(2,1)}), bf16[768,3072]{1,0:T(8,128)(2,1)}) %all-gather.11.cloned.1.call-update) | async-done | bytes 4718608 | tf_op jit(solution)/shard_map/all_gather | solution.py:496
  130.4 52.0 %all-gather.13.cloned.1.call-done.w_proj_ref = bf16[3072,768]{1,0:T(8,128)(2,1)} async-done(((bf16[384,768]{1,0:T(8,128)(2,1)}), bf16[3072,768]{1,0:T(8,128)(2,1)}) %all-gather.13.cloned.1.call-update) | async-done | bytes 4718608 | tf_op jit(solution)/shard_map/all_gather | solution.py:496
  182.5 35.5 %mlp.1 = (bf16[1024,768]{1,0:T(8,128)(2,1)}, bf16[1024,768]{1,0:T(8,128)(2,1)}, bf16[1024,3072]{1,0:T(8,128)(2,1)}, bf16[1024,768]{1,0:T(8,128)(2,1)}, bf16[1024...) custom-call(s32[4]{0:T(128)} %lengths_ref.5, ...), custom_call_target="tpu_custom_call" | custom-call | flops 21743271936 | bytes 31457280 | tf_op jit(solution)/shard_map/mlp/pallas_call | solution.py:400
  218.0 1.4 copy-done.12
  219.5 2.5 grad_out.1
  222.0 1.4 copy-done.21
  223.4 33.6 %attend_back.1 = (bf16[3,1024,768]{2,1,0:T(8,128)(2,1)}, f32[6,2,128]{2,1,0:T(2,128)S(1)}) custom-call(s32[4]{0:T(128)S(1)} %copy-done.7, s32[4]{0:T(128)S(1)} %copy-done.9, bf16[1024,2304]{1,0:T(8,128)(2,1)} %copy-done.18, bf16[1024,2304]{1,0:T(8,128)(2,1)} %copy-done.18, bf16[1024,2304]{1,0:T(8,128)(2,1)} %copy-done.18, bf16[1024,768]{1,0:T(8,128)(2,1)S(1)} %copy-done.11, ...), custom_call_target="tpu_custom_call" | custom-call | flops 16106127360 | bytes 12582912 | tf_op jit(solution)/shard_map/attend_back/pallas_call | solution.py:282
  257.0 2.3 copy-done.13
  259.3 5.4 %grad_qkv.1 = bf16[768,2304]{1,0:T(8,128)(2,1)} custom-call(bf16[1024,768]{1,0:T(8,128)(2,1)S(1)} %get-tuple-element.42.left_ref, bf16[3,1024,768]{2,1,0:T(8,128)(2,1)S(1)} %copy-done.13), custom_call_target="tpu_custom_call" | custom-call | flops 3623878656 | bytes 3538944 | tf_op jit(solution)/shard_map/grad_qkv/pallas_call | solution.py:443
  266.2 2.8 copy-done.17
  268.9 6.2 %grad_proj.1 = bf16[3072,768]{1,0:T(8,128)(2,1)S(1)} custom-call(bf16[1024,3072]{1,0:T(8,128)(2,1)S(1)} %copy-done.17, bf16[1024,768]{1,0:T(8,128)(2,1)S(1)} %copy-done.20), custom_call_target="tpu_custom_call" | custom-call | flops 4831838208 | bytes 4718592 | tf_op jit(solution)/shard_map/grad_proj/pallas_call | solution.py:443
  275.2 2.2 copy-done
  278.8 2.8 copy-done.16
  281.7 6.5 %grad_fc.1 = bf16[768,3072]{1,0:T(8,128)(2,1)S(1)} custom-call(bf16[1024,768]{1,0:T(8,128)(2,1)S(1)} %copy-done.19, bf16[1024,3072]{1,0:T(8,128)(2,1)S(1)} %copy-done.16), custom_call_target="tpu_custom_call" | custom-call | flops 4831838208 | bytes 4718592 | tf_op jit(solution)/shard_map/grad_fc/pallas_call | solution.py:443
  288.1 2.1 copy-done.1
  290.4 17.1 %reduce-scatter.5.cloned.1.call-done = bf16[96,2304]{1,0:T(8,128)(2,1)} async-done(((bf16[768,2304]{1,0:T(8,128)(2,1)}), bf16[96,2304]{1,0:T(8,128)(2,1)}) %reduce-scatter.5.cloned.1.call-update) | async-done | bytes 442384 | tf_op jit(solution)/shard_map/reduce_scatter | solution.py:500
  307.6 55.9 %reduce-scatter.11.cloned.1.call-done = bf16[384,768]{1,0:T(8,128)(2,1)} async-done(((bf16[3072,768]{1,0:T(8,128)(2,1)}), bf16[384,768]{1,0:T(8,128)(2,1)}) %reduce-scatter.11.cloned.1.call-update) | async-done | bytes 589840 | tf_op jit(solution)/shard_map/reduce_scatter | solution.py:500
  363.5 55.8 %reduce-scatter.9.cloned.1.call-done = bf16[96,3072]{1,0:T(8,128)(2,1)} async-done(((bf16[768,3072]{1,0:T(8,128)(2,1)}), bf16[96,3072]{1,0:T(8,128)(2,1)}) %reduce-scatter.9.cloned.1.call-update) | async-done | bytes 589840 | tf_op jit(solution)/shard_map/reduce_scatter | solution.py:500
  421.2 1.4 copy-done.5
  422.6 2.3 copy-done.14
  424.9 1.9 copy-done.15
  426.8 6.7 %qkv_back.1 = (bf16[1024,768]{1,0:T(8,128)(2,1)}, f32[8,768]{1,0:T(8,128)S(1)}) custom-call(bf16[1024,768]{1,0:T(8,128)(2,1)S(1)} %copy-done.5, f32[1,768]{1,0:T(1,128)S(1)} %reshape.70.gain_ref, bf16[768,2304]{1,0:T(8,128)(2,1)S(1)} %copy-done.3, bf16[3,1024,768]{2,1,0:T(8,128)(2,1)S(1)} %copy-done.14, f32[1024,768]{1,0:T(8,128)S(1)} %copy-done.15), custom_call_target="tpu_custom_call" | custom-call | flops 3623878656 | bytes 15728640 | tf_op jit(solution)/shard_map/qkv_back/pallas_call | solution.py:475
  433.7 26.0 %all-reduce.9 = (bf16[768]{0:T(1024)(128)(2,1)S(1)}, bf16[768]{0:T(1024)(128)(2,1)S(1)}, bf16[768]{0:T(1024)(128)(2,1)S(1)}, bf16[768]{0:T(1024)(128)(2,1)S(1)},...) all-reduce(bf16[768]{0:T(1024)(128)(2,1)S(1)} %get-tuple-element.89, ...), channel_id=3, replica_groups=mesh['rep'=4,'shard'=8] {'shard'}, use_global_device_ids=true, to_apply=%region_0.0.clone | all-reduce | flops 9216 | bytes 36864
  460.3 9.9 %all-reduce.10 = (bf16[96]{0:T(256)(128)(2,1)S(1)}, bf16[96]{0:T(256)(128)(2,1)S(1)}, bf16[96]{0:T(256)(128)(2,1)S(1)}, bf16[96]{0:T(256)(128)(2,1)S(1)}, bf16[9...) all-reduce(bf16[96]{0:T(256)(128)(2,1)S(1)} %dynamic-slice.1, ...), channel_id=1, replica_groups=mesh['rep'=4,'shard'=8] {'rep'}, use_global_device_ids=true, to_apply=%region_1.0 | all-reduce | flops 1152 | bytes 4608 | tf_op jit(solution)/shard_map/psum | solution.py:501
  475.0 11.4 %all-reduce.14.cloned.1.call-done = (bf16[96,2304]{1,0:T(8,128)(2,1)}, bf16[96,768]{1,0:T(8,128)(2,1)}, bf16[96,3072]{1,0:T(8,128)(2,1)}, bf16[384,768]{1,0:T(8,128)(2,1)}) async-done(((bf16[96,2304]{1,0:T(8,128)(2,1)}, bf16[96,768]{1,0:T(8,128)(2,1)}, bf16[96,3072]{1,0:T(8,128)(2,1)}, bf16[384,768]{1,0:T(8,128)(2,1)}), (bf16[96,2304]{1,0:T(8,128)(2,1)}, bf16[96,768]{1,0:T(8,128)(2,1)}, ...) | async-done | bytes 1769488 | tf_op jit(solution)/shard_map/psum | solution.py:501
  486.4 2.2 convert_element_type.101
  (127 shorter events, 19.7 us)
Async XLA Ops:
  7.2 2.9 copy-start.28
  7.2 2.9 copy-start.29
  7.2 2.9 copy-start.30
  7.2 2.9 copy-start.31
  7.2 2.9 copy-start.32
  7.2 2.9 copy-start.33
  7.2 2.9 copy-start.34
  7.3 2.9 copy-start.27
  7.3 2.9 copy-start.35
  7.3 46.8 %copy-start.4 = (bf16[1024,768]{1,0:T(8,128)(2,1)S(1)}, bf16[1024,768]{1,0:T(8,128)(2,1)}, u32[]{:S(2)}) copy-start(bf16[1024,768]{1,0:T(8,128)(2,1)} %x_ref.5) | copy-start | bytes 4718596
  7.3 46.8 %all-gather.7.cloned.1.call-start = ((), (), s32[]{:S(2)}) async-start(), calls=%async_computation.4 | async-start | bytes 3981312 | tf_op jit(solution)/shard_map/all_gather | solution.py:496
  8.0 80.9 %all-gather.9.cloned.1.call-start = ((), (), s32[]{:S(2)}) async-start(), calls=%async_computation.5 | async-start | bytes 1327104 | tf_op jit(solution)/shard_map/all_gather | solution.py:496
  8.8 121.7 %all-gather.11.cloned.1.call-start = ((), (), s32[]{:S(2)}) async-start(), calls=%async_computation.6 | async-start | bytes 5308416 | tf_op jit(solution)/shard_map/all_gather | solution.py:496
  9.5 173.0 %all-gather.13.cloned.1.call-start = ((), (), s32[]{:S(2)}) async-start(), calls=%async_computation.7 | async-start | bytes 5308416 | tf_op jit(solution)/shard_map/all_gather | solution.py:496
  10.1 280.3 %reduce-scatter.7.cloned.1.call-start = ((), (), s32[]{:S(2)}) async-start(), calls=%async_computation.9 | async-start | bytes 1327104 | tf_op jit(solution)/shard_map/reduce_scatter | solution.py:500
  56.1 5.3 %copy-start.6 = (s32[4]{0:T(128)S(1)}, s32[4]{0:T(128)}, u32[]{:S(2)}) copy-start(s32[4]{0:T(128)} %lengths_ref.5) | copy-start | bytes 52
  56.1 5.3 %copy-start.8 = (s32[4]{0:T(128)S(1)}, s32[4]{0:T(128)}, u32[]{:S(2)}) copy-start(s32[4]{0:T(128)} %blocks_ref.5) | copy-start | bytes 52
  182.5 35.5 %copy-start.11 = (bf16[1024,768]{1,0:T(8,128)(2,1)S(1)}, bf16[1024,768]{1,0:T(8,128)(2,1)}, u32[]{:S(2)}) copy-start(bf16[1024,768]{1,0:T(8,128)(2,1)} %copy-done.10) | copy-start | bytes 4718596
  219.4 2.5 copy-start.7
  219.4 2.5 copy-start.9
  221.9 85.6 %reduce-scatter.5.cloned.1.call-start = ((), (), s32[]{:S(2)}) async-start(), calls=%async_computation.8 | async-start | bytes 3981312 | tf_op jit(solution)/shard_map/reduce_scatter | solution.py:500
  264.8 98.7 %reduce-scatter.11.cloned.1.call-start = ((), (), s32[]{:S(2)}) async-start(), calls=%async_computation.11 | async-start | bytes 5308416 | tf_op jit(solution)/shard_map/reduce_scatter | solution.py:500
  266.2 2.8 copy-start.17
  277.4 141.8 %reduce-scatter.9.cloned.1.call-start = ((), (), s32[]{:S(2)}) async-start(), calls=%async_computation.10 | async-start | bytes 5308416 | tf_op jit(solution)/shard_map/reduce_scatter | solution.py:500
  278.8 2.8 copy-start.16
  290.3 130.9 %copy-start.3 = (bf16[768,2304]{1,0:T(8,128)(2,1)S(1)}, bf16[768,2304]{1,0:T(8,128)(2,1)}, u32[]{:S(2)}) copy-start(bf16[768,2304]{1,0:T(8,128)(2,1)} %all-gather.7.cloned.1.call-done.w_ref) | copy-start | bytes 10616836
  290.3 128.9 %copy-start.36 = (u32[32]{0:T(128)S(1)}, u32[32]{0:T(128)}, u32[]{:S(2)}) copy-start(u32[32]{0:T(128)} %constant.6) | copy-start | bytes 388
  290.3 196.1 %all-reduce.14.cloned.1.call-start = ((), (), s32[]{:S(2)}) async-start(), calls=%async_computation.12 | async-start | bytes 3538944 | tf_op jit(solution)/shard_map/psum | solution.py:501
  422.6 2.3 copy-start.14
  426.8 6.7 %copy-start.25 = (f32[8,768]{1,0:T(8,128)S(1)}, f32[8,768]{1,0:T(8,128)}, u32[]{:S(2)}) copy-start(f32[8,768]{1,0:T(8,128)} %get-tuple-element.45) | copy-start | bytes 73732
  426.8 6.7 %copy-start.26 = (f32[1,3072]{1,0:T(1,128)S(1)}, f32[1,3072]{1,0:T(1,128)}, u32[]{:S(2)}) copy-start(f32[1,3072]{1,0:T(1,128)} %get-tuple-element.48) | copy-start | bytes 36868
  486.4 3.4 copy-start.23
  (14 other events, 25.4 us)
Sparse Core Ops, SparseCore 0:
  9.8 44.2 all-gather.6
  55.7 21.5 all-gather.8
  78.9 51.4 all-gather.10
  131.9 50.5 all-gather.12
  222.0 31.4 reduce-scatter.6
  264.9 42.6 reduce-scatter.4
  310.0 53.4 reduce-scatter.10
  365.9 53.3 reduce-scatter.8
  423.1 63.2 all-reduce.13
